TPU v7x, 32 devices: a whole 2x2x4 slice. The times are simulated.
32 devices in a mesh: rows: 8 (over z, x), rank: 4 (over y, core).
Axes of the slice: x: 2, y: 2, z: 4, core: 2. Of those that a mesh axis runs over, the one named last changes fastest.
Arguments:
- tokens: bfloat16 [32768, 768], P(('rows', 'rank')), may hold values from -6 to 6
- w_query: bfloat16 [768, 768], P('rows'), may hold values from -0.21875 to 0.21875
- w_key: bfloat16 [768, 768], P('rows'), may hold values from -0.21875 to 0.21875
- w_value: bfloat16 [768, 768], P('rows'), may hold values from -0.21875 to 0.21875
- w_out: bfloat16 [768, 768], P('rows'), may hold values from -1.25 to 1.25
- w_up: bfloat16 [768, 3072], P('rows'), may hold values from -0.21875 to 0.21875
- w_down: bfloat16 [3072, 768], P('rows'), may hold values from -0.109375 to 0.109375
- gain_one: float32 [768], replicated, may hold values from 0.5 to 1.5
- shift_one: float32 [768], replicated, may hold values from -1.5 to 1.5
- gain_two: float32 [768], replicated, may hold values from 0.5 to 1.5
- shift_two: float32 [768], replicated, may hold values from -1.5 to 1.5
- adapter_a: bfloat16 [768, 1024], P(None, 'rank'), may hold values from -0.21875 to 0.21875
- adapter_b: bfloat16 [1024, 768], P('rank'), may hold values from -0.1875 to 0.1875
- query_rank_scale: bfloat16 [1024], P('rank'), may hold values from 0.29882812 to 1.5
- value_rank_scale: bfloat16 [1024], P('rank'), may hold values from 0.29882812 to 1.5
- query_out_scale: bfloat16 [768], replicated, may hold values from -4 to 4
- value_out_scale: bfloat16 [768], replicated, may hold values from -4 to 4
- segments: int32 [64, 512], P(('rows', 'rank')), may hold values from 0 to 15, never falling along the last dimension, each value on 1 to 128 neighbouring positions
- cotangent: bfloat16 [32768, 768], P(('rows', 'rank')), may hold values from -6 to 6
Outputs:
- layer_out: bfloat16 [32768, 768], P(('rows', 'rank'))
- input_grad: bfloat16 [32768, 768], P(('rows', 'rank'))
- grad_query_rank: float32 [1024], P('rank')
- grad_value_rank: float32 [1024], P('rank')
- grad_query_out: float32 [768], replicated
- grad_value_out: float32 [768], replicated
Inputs may be any that keep to these rules, and one draw needn't show every extreme that they name: `segments`: segment numbers never fall along a packed row of 512 tokens; a token attends only to tokens of its own row and segment.
All inputs are finite; a program needn't handle non-finite values.
Results may differ from a plain program's by a relative error of at most 0.029.
Values may be sent and summed in bfloat16 or wider, within the bound.
A program may use at most 192 MiB of HBM per device.

v0:
```python
from functools import partial
import math

import jax
import jax.numpy as jnp
from jax import lax
from jax.sharding import PartitionSpec as P

HEADS = 12
HEAD = 64


epsilon = 1e-05
masked_score = -1e30


def norm_forward(stream, norm_gain, norm_shift):
    centered = stream - jnp.mean(stream, axis=-1, keepdims=True)
    inverse = lax.rsqrt(jnp.mean(centered * centered, axis=-1, keepdims=True) + epsilon)
    normed = centered * inverse
    return (normed * norm_gain + norm_shift, normed, inverse)


def norm_backward(upstream, normed, inverse, norm_gain):
    scaled = upstream * norm_gain
    mean_grad = jnp.mean(scaled, axis=-1, keepdims=True)
    mean_cross = jnp.mean(scaled * normed, axis=-1, keepdims=True)
    return inverse * (scaled - mean_grad - normed * mean_cross)


def transpose_dot(operand, matrix):
    return lax.dot_general(
        operand, matrix, (((1,), (1,)), ((), ())), preferred_element_type=jnp.float32
    )


def head_scores(query_heads, key_heads, segment_ids):
    scores = jnp.einsum(
        "qhd,khd->hqk", query_heads, key_heads, preferred_element_type=jnp.float32
    ) / math.sqrt(HEAD)
    same_doc = segment_ids[:, None] == segment_ids[None, :]
    return jnp.where(same_doc[None], scores, masked_score)


def attend_forward(pieces):
    query_heads, key_heads, value_heads, segment_ids = pieces
    scores = head_scores(query_heads, key_heads, segment_ids)
    row_peak = jnp.max(scores, axis=-1, keepdims=True)
    weights = jnp.exp(scores - row_peak)
    row_total = jnp.sum(weights, axis=-1, keepdims=True)
    attention = weights / row_total
    mixture = jnp.einsum(
        "hqk,khd->qhd",
        attention.astype(jnp.bfloat16),
        value_heads,
        preferred_element_type=jnp.float32,
    )
    return (mixture, row_peak + jnp.log(row_total))


def attend_backward(pieces):
    query_heads, key_heads, value_heads, grad_heads, segment_ids, log_total = pieces
    scores = head_scores(query_heads, key_heads, segment_ids)
    attention = jnp.exp(scores - log_total)
    grad_attn = jnp.einsum(
        "qhd,khd->hqk", grad_heads, value_heads, preferred_element_type=jnp.float32
    )
    centre = jnp.sum(attention * grad_attn, axis=-1, keepdims=True)
    grad_scores = (attention * (grad_attn - centre)).astype(jnp.bfloat16)
    grad_query = (
        jnp.einsum("hqk,khd->qhd", grad_scores, key_heads, preferred_element_type=jnp.float32)
        / math.sqrt(HEAD)
    ).astype(jnp.bfloat16)
    grad_key = (
        jnp.einsum("hqk,qhd->khd", grad_scores, query_heads, preferred_element_type=jnp.float32)
        / math.sqrt(HEAD)
    ).astype(jnp.bfloat16)
    grad_value = jnp.einsum(
        "hqk,qhd->khd",
        attention.astype(jnp.bfloat16),
        grad_heads,
        preferred_element_type=jnp.float32,
    ).astype(jnp.bfloat16)
    return (grad_query, grad_key, grad_value)


def per_device(
    tokens,
    w_query,
    w_key,
    w_value,
    w_out,
    w_up,
    w_down,
    gain_one,
    shift_one,
    gain_two,
    shift_two,
    adapter_a,
    adapter_b,
    query_rank_scale,
    value_rank_scale,
    query_out_scale,
    value_out_scale,
    segments,
    cotangent,
):
    local_rows = tokens.shape[0]
    width = tokens.shape[1]
    rows_here = segments.shape[0]
    row_length = segments.shape[1]

    def split_heads(tensor_rows):
        return tensor_rows.reshape(rows_here, row_length, HEADS, HEAD)

    full_query, full_key, full_value, full_out, full_up, full_down = (
        lax.all_gather(w_query, "rows", axis=0, tiled=True),
        lax.all_gather(w_key, "rows", axis=0, tiled=True),
        lax.all_gather(w_value, "rows", axis=0, tiled=True),
        lax.all_gather(w_out, "rows", axis=0, tiled=True),
        lax.all_gather(w_up, "rows", axis=0, tiled=True),
        lax.all_gather(w_down, "rows", axis=0, tiled=True),
    )
    group_tokens = lax.all_gather(tokens, "rank", axis=0, tiled=True)
    hidden_rank = jnp.dot(group_tokens, adapter_a, preferred_element_type=jnp.float32)
    ranked_query = (hidden_rank * query_rank_scale).astype(jnp.bfloat16)
    ranked_value = (hidden_rank * value_rank_scale).astype(jnp.bfloat16)
    both_parts = lax.psum_scatter(
        jnp.concatenate(
            [
                jnp.dot(ranked_query, adapter_b, preferred_element_type=jnp.float32),
                jnp.dot(ranked_value, adapter_b, preferred_element_type=jnp.float32),
            ],
            axis=1,
        ).astype(jnp.bfloat16),
        "rank",
        scatter_dimension=0,
        tiled=True,
    ).astype(jnp.float32)
    part_query = both_parts[:, :width]
    part_value = both_parts[:, width:]
    queries = (
        jnp.dot(tokens, full_query, preferred_element_type=jnp.float32)
        + part_query * query_out_scale
    ).astype(jnp.bfloat16)
    key_rows = jnp.dot(tokens, full_key, preferred_element_type=jnp.float32).astype(jnp.bfloat16)
    values = (
        jnp.dot(tokens, full_value, preferred_element_type=jnp.float32)
        + part_value * value_out_scale
    ).astype(jnp.bfloat16)
    mixture, log_total = lax.map(
        attend_forward, (split_heads(queries), split_heads(key_rows), split_heads(values), segments)
    )
    mixture_low = mixture.reshape(local_rows, width).astype(jnp.bfloat16)
    first_sum = tokens.astype(jnp.float32) + jnp.dot(
        mixture_low, full_out, preferred_element_type=jnp.float32
    )
    normed_out, normed_one, inverse_one = norm_forward(first_sum, gain_one, shift_one)
    up_proj = jnp.dot(normed_out.astype(jnp.bfloat16), full_up, preferred_element_type=jnp.float32)
    activated = jax.nn.gelu(up_proj, approximate=False).astype(jnp.bfloat16)
    second_sum = normed_out + jnp.dot(activated, full_down, preferred_element_type=jnp.float32)
    layer_out, normed_two, inverse_two = norm_forward(second_sum, gain_two, shift_two)
    full_query, full_key, full_value, full_out, full_up, full_down = (
        lax.all_gather(w_query, "rows", axis=0, tiled=True),
        lax.all_gather(w_key, "rows", axis=0, tiled=True),
        lax.all_gather(w_value, "rows", axis=0, tiled=True),
        lax.all_gather(w_out, "rows", axis=0, tiled=True),
        lax.all_gather(w_up, "rows", axis=0, tiled=True),
        lax.all_gather(w_down, "rows", axis=0, tiled=True),
    )
    grad_second = norm_backward(cotangent.astype(jnp.float32), normed_two, inverse_two, gain_two)
    grad_act = transpose_dot(grad_second.astype(jnp.bfloat16), full_down)
    gelu_grad = jax.vjp(partial(jax.nn.gelu, approximate=False), up_proj)[1](grad_act)[0]
    grad_normed = grad_second + transpose_dot(gelu_grad.astype(jnp.bfloat16), full_up)
    grad_first = norm_backward(grad_normed, normed_one, inverse_one, gain_one)
    grad_mixture = transpose_dot(grad_first.astype(jnp.bfloat16), full_out).astype(jnp.bfloat16)
    grad_query, grad_key, grad_value = lax.map(
        attend_backward,
        (
            split_heads(queries),
            split_heads(key_rows),
            split_heads(values),
            split_heads(grad_mixture),
            segments,
            log_total,
        ),
    )
    grad_query = grad_query.reshape(local_rows, width)
    grad_key = grad_key.reshape(local_rows, width)
    grad_value = grad_value.reshape(local_rows, width)
    input_sum = (
        grad_first
        + transpose_dot(grad_query, full_query)
        + transpose_dot(grad_key, full_key)
        + transpose_dot(grad_value, full_value)
    )
    out_query = grad_query * query_out_scale
    out_value = grad_value * value_out_scale
    scale_query_part = jnp.sum(grad_query * part_query, axis=0)
    scale_value_part = jnp.sum(grad_value * part_value, axis=0)
    group_query, group_value = (
        lax.all_gather(out_query, "rank", axis=0, tiled=True),
        lax.all_gather(out_value, "rank", axis=0, tiled=True),
    )
    rank_query = transpose_dot(group_query, adapter_b)
    rank_value = transpose_dot(group_value, adapter_b)
    rank_query_part = jnp.sum(hidden_rank * rank_query, axis=0)
    rank_value_part = jnp.sum(hidden_rank * rank_value, axis=0)
    grad_hidden = (rank_query * query_rank_scale + rank_value * value_rank_scale).astype(
        jnp.bfloat16
    )
    input_sum = input_sum + lax.psum_scatter(
        transpose_dot(grad_hidden, adapter_a).astype(jnp.bfloat16),
        "rank",
        scatter_dimension=0,
        tiled=True,
    ).astype(jnp.float32)
    grad_query_rank, grad_value_rank = lax.psum((rank_query_part, rank_value_part), "rows")
    grad_query_out, grad_value_out = lax.psum(
        (scale_query_part, scale_value_part), ("rows", "rank")
    )
    return (
        layer_out.astype(jnp.bfloat16),
        input_sum.astype(jnp.bfloat16),
        grad_query_rank,
        grad_value_rank,
        grad_query_out,
        grad_value_out,
    )


def solution(mesh):
    return jax.shard_map(
        per_device,
        mesh=mesh,
        in_specs=(
            P(("rows", "rank"), None),
            P("rows", None),
            P("rows", None),
            P("rows", None),
            P("rows", None),
            P("rows", None),
            P("rows", None),
            P(),
            P(),
            P(),
            P(),
            P(None, "rank"),
            P("rank", None),
            P("rank"),
            P("rank"),
            P(),
            P(),
            P(("rows", "rank"), None),
            P(("rows", "rank"), None),
        ),
        out_specs=(
            P(("rows", "rank"), None),
            P(("rows", "rank"), None),
            P("rank"),
            P("rank"),
            P(),
            P(),
        ),
        check_vma=False,
    )
```

profile of v0, /device:TPU:0, one launch (start us, length us, event | category | flops | bytes accessed | tf_op | source)
XLA Modules:
  0.0 817.2 jit_solution(3723644811276019653)
XLA Ops:
  10.0 48.7 %all-gather.12.cloned.1.call-done = bf16[4096,768]{1,0:T(8,128)(2,1)} async-done(((bf16[1024,768]{1,0:T(8,128)(2,1)}), bf16[4096,768]{1,0:T(8,128)(2,1)}) %all-gather.12.cloned.1.call-update) | async-done | bytes 6291472 | tf_op jit(solution)/shard_map/all_gather | solution.py:124
  58.7 4.6 fusion.92
  63.4 1.8 convolution_convert_fusion.1
  65.3 1.8 convolution_convert_fusion.2
  67.1 5.4 pad_maximum_fusion
  79.4 22.6 %all-gather.16.cloned.1.call-done = bf16[768,768]{1,0:T(8,128)(2,1)} async-done(((bf16[96,768]{1,0:T(8,128)(2,1)}), bf16[768,768]{1,0:T(8,128)(2,1)}) %all-gather.16.cloned.1.call-update) | async-done | bytes 1179664 | tf_op jit(solution)/shard_map/all_gather | solution.py:118
  102.0 3.8 convolution_convert_fusion.4
  107.5 2.4 reshape.176
  111.6 90.8 %reduce-scatter.3.cloned.1.call-done = bf16[1024,1536]{1,0:T(8,128)(2,1)} async-done(((bf16[4096,1536]{1,0:T(8,128)(2,1)}), bf16[1024,1536]{1,0:T(8,128)(2,1)}) %reduce-scatter.3.cloned.1.call-update) | async-done | bytes 3145744 | tf_op jit(solution)/shard_map/reduce_scatter | solution.py:128
  202.4 5.4 convert_element_type.116
  207.9 37.7 %all-gather.10.cloned.1.call-done = bf16[768,768]{1,0:T(8,128)(2,1)} async-done(((bf16[96,768]{1,0:T(8,128)(2,1)}), bf16[768,768]{1,0:T(8,128)(2,1)}) %all-gather.10.cloned.1.call-update) | async-done | bytes 1179664 | tf_op jit(solution)/shard_map/all_gather | solution.py:119
  245.5 4.8 add_convert_fusion.6
  250.3 2.6 copy.55
  252.9 3.9 reshape.174
  256.8 2.9 copy.58
  259.7 27.8 %all-gather.14.cloned.1.call-done = bf16[768,768]{1,0:T(8,128)(2,1)} async-done(((bf16[96,768]{1,0:T(8,128)(2,1)}), bf16[768,768]{1,0:T(8,128)(2,1)}) %all-gather.14.cloned.1.call-update) | async-done | bytes 1179664 | tf_op jit(solution)/shard_map/all_gather | solution.py:117
  287.4 4.8 add_convert_fusion.5
  294.0 2.4 reshape.175
  298.1 24.3 %while.26 = (s32[]{:T(128)}, bf16[2,512,12,64]{1,3,2,0:T(8,128)(2,1)}, f32[2,12,512,1]{2,1,3,0:T(8,128)}, bf16[2,512,12,64]{1,3,2,0:T(8,128)(2,1)}, s32[2,512]{1...) while((s32[]{:T(128)}, ...), condition=%wide.region_4.5_spmd, body=%wide.region_1.4_spmd.sunk | while | flops 843311104 | bytes 43991668 | solution.py:151
  298.6 2.1 fusion.142
  300.7 3.5 fusion.143
  304.8 5.5 bitcast_dynamic-update-slice_fusion.4
  310.6 2.1 fusion.142
  312.6 3.6 fusion.143
  316.9 5.5 bitcast_dynamic-update-slice_fusion.4
  322.3 3.0 copy.61
  327.0 2.4 all-gather.18.cloned.1.call-done
  329.3 3.8 fusion.88
  335.2 75.0 %all-gather.20.cloned.1.call-done = bf16[768,3072]{1,0:T(8,128)(2,1)} async-done(((bf16[96,3072]{1,0:T(8,128)(2,1)}), bf16[768,3072]{1,0:T(8,128)(2,1)}) %all-gather.20.cloned.1.call-update) | async-done | bytes 4718608 | tf_op jit(solution)/shard_map/all_gather | solution.py:121
  410.2 36.3 %fusion.54 = (f32[1024,3072]{1,0:T(8,128)}, f32[1024,3072]{1,0:T(8,128)}) fusion(bf16[768,3072]{1,0:T(8,128)(2,1)} %all-gather.20.cloned.1.call-done, f32[1024,768]{0,1:T(8,128)} %copy-done.8, f32[768]{0:T(1024)} %param.31, f32[768]{0:T(1024)} %param.30, f32[1024]{0:T(1024)S(1)} %add_rsqrt_fusion.1, f32[1024]{0:T(1024)S(1)} %broadcast_multiply_fusion.7), kind=kOutput, calls=%fused_computation.63 | convolution fusion | flops 5030805504 | bytes 33044480 | tf_op jit(solution)/shard_map/dot_general | solution.py:159
  446.5 43.9 %all-gather.22.cloned.1.call-done = bf16[3072,768]{1,0:T(8,128)(2,1)} async-done(((bf16[384,768]{1,0:T(8,128)(2,1)}), bf16[3072,768]{1,0:T(8,128)(2,1)}) %all-gather.22.cloned.1.call-update) | async-done | bytes 4718608 | tf_op jit(solution)/shard_map/all_gather | solution.py:122
  490.4 15.7 %fusion.89 = (f32[1024]{0:T(1024)}, f32[1024,768]{0,1:T(8,128)}) fusion(bf16[3072,768]{1,0:T(8,128)(2,1)} %all-gather.22.cloned.1.call-done, f32[1024,3072]{1,0:T(8,128)} %get-tuple-element.202, f32[1024,3072]{1,0:T(8,128)} %get-tuple-element.203, f32[768]{0:T(1024)S(1)} %copy-done.41, f32[768]{0:T(1024)} %param.30, f32[1024]{0:T(1024)S(1)} %add_rsqrt_fusion.1, ...), kind=kOutput, calls=%fused_computation.142 | convolution fusion | flops 4845992960 | bytes 36194304 | tf_op jit(solution)/shard_map/dot_general | solution.py:161
  507.0 2.4 multiply_reduce_fusion.7
  509.5 3.6 fusion.63
  513.7 24.6 %fusion.87 = (f32[1024]{0:T(1024)}, f32[1024]{0:T(1024)}, f32[1024,768]{0,1:T(8,128)}) fusion(f32[1024]{0:T(1024)} %copy-done.22, f32[1024,768]{0,1:T(8,128)} %copy-done.8, f32[1024]{0:T(1024)S(1)} %broadcast_multiply_fusion.7, f32[768]{0:T(1024)} %param.30, bf16[768,3072]{1,0:T(8,128)(2,1)} %all-gather.20.cloned.1.call-done, ...), kind=kOutput, calls=%fused_computation.140 | convolution fusion | flops 9726588928 | bytes 45651968 | tf_op jit(solution)/shard_map/dot_general | solution.py:32
  540.2 6.4 convolution_convert_fusion.3
  546.6 2.6 copy.63
  549.2 3.8 reshape.177
  553.0 2.9 copy.66
  555.9 49.1 %while.27 = (s32[]{:T(128)}, bf16[2,512,12,64]{1,3,2,0:T(8,128)(2,1)}, bf16[2,512,12,64]{1,3,2,0:T(8,128)(2,1)}, bf16[2,512,12,64]{1,3,2,0:T(8,128)(2,1)}, bf16[...) while((s32[]{:T(128)}, ...), condition=%wide.region_15.16_spmd, body=%wide.region_13.15_spmd.sunk | while | flops 2062673920 | bytes 147721584 | solution.py:177
  556.1 1.8 fusion.152
  558.3 6.9 multiply_reduce_fusion.10
  565.1 7.1 multiply_convert_fusion.12
  572.3 2.0 fusion.154
  576.7 3.9 fusion.155
  580.6 1.8 fusion.152
  582.7 6.9 multiply_reduce_fusion.10
  589.6 7.1 multiply_convert_fusion.12
  596.7 2.0 fusion.154
  601.1 3.9 fusion.155
  605.0 3.0 copy.68
  613.9 40.6 %all-gather.24.cloned.1.call-done = bf16[4096,768]{0,1:T(8,128)(2,1)} async-done(((bf16[1024,768]{0,1:T(8,128)(2,1)}), bf16[4096,768]{0,1:T(8,128)(2,1)}) %all-gather.24.cloned.1.call-update) | async-done | bytes 6291472 | tf_op jit(solution)/shard_map/all_gather | solution.py:202
  654.5 6.6 fusion.93
  661.1 41.8 %all-gather.26.cloned.1.call-done = bf16[4096,768]{0,1:T(8,128)(2,1)} async-done(((bf16[1024,768]{0,1:T(8,128)(2,1)}), bf16[4096,768]{0,1:T(8,128)(2,1)}) %all-gather.26.cloned.1.call-update) | async-done | bytes 6291472 | tf_op jit(solution)/shard_map/all_gather | solution.py:203
  703.0 8.2 %multiply_reduce_fusion.1 = (f32[256]{0:T(256)}, f32[256]{0:T(256)}, f32[4096,256]{1,0:T(8,128)S(1)}) fusion(f32[4096,256]{1,0:T(8,128)} %copy-done.1, f32[4096,256]{1,0:T(8,128)} %fusion.93, bf16[4096,768]{0,1:T(8,128)(2,1)} %all-gather.26.cloned.1.call-done, bf16[256,768]{1,0:T(8,128)(2,1)S(1)} %copy-done), kind=kOutput, calls=%fused_computation.86 | convolution fusion | flops 1614806528 | bytes 19269632 | tf_op jit(solution)/shard_map/dot_general | solution.py:32
  711.2 4.5 convolution_convert_fusion
  718.9 3.0 copy.70
  723.5 2.9 copy.77
  726.3 4.9 multiply_reduce_fusion.3
  731.2 40.5 %all-reduce = (f32[768]{0:T(1024)}, f32[768]{0:T(1024)}) all-reduce(f32[768]{0:T(1024)S(1)} %get-tuple-element.150, f32[768]{0:T(1024)S(1)} %get-tuple-element.149), channel_id=1, replica_groups=mesh['rows'=8,'rank'=4] {'rows','rank'}, use_global_device_ids=true, to_apply=%region_22.23 | all-reduce | flops 1536 | bytes 12288 | tf_op jit(solution)/shard_map/psum | solution.py:219
  771.8 4.5 fusion.94
  776.3 3.1 fusion.95
  779.4 21.6 %all-reduce.1 = (f32[256]{0:T(256)}, f32[256]{0:T(256)}) all-reduce(f32[256]{0:T(256)S(1)} %copy-done.39, f32[256]{0:T(256)S(1)} %copy-done.38), channel_id=1, replica_groups=mesh['rows'=8,'rank'=4] {'rows'}, use_global_device_ids=true, to_apply=%region_18.19 | all-reduce | flops 512 | bytes 4096 | tf_op jit(solution)/shard_map/psum | solution.py:218
  801.0 7.5 add_convert_fusion.3
  (172 shorter events, 42.6 us)
Async XLA Ops:
  7.2 56.2 %copy-start = (bf16[256,768]{1,0:T(8,128)(2,1)S(1)}, bf16[256,768]{1,0:T(8,128)(2,1)}, u32[]{:S(2)}) copy-start(bf16[256,768]{1,0:T(8,128)(2,1)} %param.35) | copy-start | bytes 1179652
  7.2 51.5 %all-gather.12.cloned.1.call-start = ((), (), s32[]{:S(2)}) async-start(), calls=%async_computation.3 | async-start | bytes 7864320 | tf_op jit(solution)/shard_map/all_gather | solution.py:124
  7.9 94.0 %all-gather.16.cloned.1.call-start = ((), (), s32[]{:S(2)}) async-start(), calls=%async_computation.6 | async-start | bytes 1327104 | tf_op jit(solution)/shard_map/all_gather | solution.py:118
  8.7 193.8 %reduce-scatter.3.cloned.1.call-start = ((), (), s32[]{:S(2)}) async-start(), calls=%async_computation.4 | async-start | bytes 15728640 | tf_op jit(solution)/shard_map/reduce_scatter | solution.py:128
  9.4 54.0 %copy-start.28 = (f32[256]{0:T(256)}, f32[256]{0:T(256)S(1)}, u32[]{:S(2)}) copy-start(f32[256]{0:T(256)S(1)} %convert_element_type.114) | copy-start | bytes 3076
  10.0 55.1 %copy-start.30 = (f32[256]{0:T(256)}, f32[256]{0:T(256)S(1)}, u32[]{:S(2)}) copy-start(f32[256]{0:T(256)S(1)} %convert_element_type.112) | copy-start | bytes 3076
  63.3 1.9 copy-start.1
  72.5 3.6 copy-start.9
  72.5 5.2 copy-start.34
  72.5 5.2 copy-start.32
  72.6 5.2 copy-start.10
  72.6 173.0 %all-gather.10.cloned.1.call-start = ((), (), s32[]{:S(2)}) async-start(), calls=%async_computation.2 | async-start | bytes 1327104 | tf_op jit(solution)/shard_map/all_gather | solution.py:119
  73.2 214.3 %all-gather.14.cloned.1.call-start = ((), (), s32[]{:S(2)}) async-start(), calls=%async_computation.5 | async-start | bytes 1327104 | tf_op jit(solution)/shard_map/all_gather | solution.py:117
  73.7 255.6 %all-gather.18.cloned.1.call-start = ((), (), s32[]{:S(2)}) async-start(), calls=%async_computation.7 | async-start | bytes 1327104 | tf_op jit(solution)/shard_map/all_gather | solution.py:120
  74.3 335.9 %all-gather.20.cloned.1.call-start = ((), (), s32[]{:S(2)}) async-start(), calls=%async_computation.8 | async-start | bytes 5308416 | tf_op jit(solution)/shard_map/all_gather | solution.py:121
  75.1 415.4 %all-gather.22.cloned.1.call-start = ((), (), s32[]{:S(2)}) async-start(), calls=%async_computation.9 | async-start | bytes 5308416 | tf_op jit(solution)/shard_map/all_gather | solution.py:122
  75.8 578.7 %all-gather.24.cloned.1.call-start = ((), (), s32[]{:S(2)}) async-start(), calls=%async_computation.10 | async-start | bytes 7864320 | tf_op jit(solution)/shard_map/all_gather | solution.py:202
  294.0 4.1 copy-start.19
  298.6 2.1 copy-start.3
  310.6 2.1 copy-start.3
  333.1 1.7 copy-start.8
  333.1 206.5 %copy-start.20 = (f32[1024]{0:T(1024)}, f32[1024]{0:T(1024)S(1)}, u32[]{:S(2)}) copy-start(f32[1024]{0:T(1024)S(1)} %broadcast_multiply_fusion.7) | copy-start | bytes 12292
  335.2 155.3 %copy-start.22 = (f32[1024]{0:T(1024)}, f32[1024]{0:T(1024)S(1)}, u32[]{:S(2)}) copy-start(f32[1024]{0:T(1024)S(1)} %add_rsqrt_fusion.1) | copy-start | bytes 12292
  335.2 155.3 %copy-start.41 = (f32[768]{0:T(1024)S(1)}, f32[768]{0:T(1024)}, u32[]{:S(2)}) copy-start(f32[768]{0:T(1024)} %param.31) | copy-start | bytes 9220
  506.2 3.3 copy-start.7
  506.2 3.3 copy-start.36
  506.2 3.3 copy-start.37
  539.0 7.7 copy-start.24
  539.7 0.6 copy-start.26
  556.1 2.1 copy-start.18
  556.1 2.1 copy-start.4
  556.1 2.1 copy-start.5
  565.1 7.1 copy-start.13
  572.3 2.0 copy-start.11
  574.3 1.2 copy-start.14
  574.3 2.4 copy-start.6
  575.5 1.2 copy-start.12
  580.6 2.1 copy-start.18
  580.6 2.1 copy-start.4
  580.6 2.1 copy-start.5
  589.6 7.1 copy-start.13
  596.7 2.0 copy-start.11
  598.7 1.2 copy-start.14
  598.7 2.4 copy-start.6
  599.9 1.2 copy-start.12
  605.0 3.5 copy-start.33
  608.5 2.0 copy-start.15
  609.9 93.1 %all-gather.26.cloned.1.call-start = ((), (), s32[]{:S(2)}) async-start(), calls=%async_computation.11 | async-start | bytes 7864320 | tf_op jit(solution)/shard_map/all_gather | solution.py:203
  610.5 2.0 copy-start.35
  613.9 187.1 %reduce-scatter.5.cloned.1.call-start = ((), (), s32[]{:S(2)}) async-start(), calls=%async_computation.12 | async-start | bytes 7864320 | tf_op jit(solution)/shard_map/reduce_scatter | solution.py:212
  661.1 50.1 %copy-start.29 = (f32[256]{0:T(256)S(1)}, f32[256]{0:T(256)}, u32[]{:S(2)}) copy-start(f32[256]{0:T(256)} %copy-done.28) | copy-start | bytes 3076
  661.1 50.1 %copy-start.31 = (f32[256]{0:T(256)S(1)}, f32[256]{0:T(256)}, u32[]{:S(2)}) copy-start(f32[256]{0:T(256)} %copy-done.30) | copy-start | bytes 3076
  702.9 8.2 %copy-start.2 = (f32[4096,256]{1,0:T(8,128)S(1)}, f32[4096,256]{1,0:T(8,128)}, u32[]{:S(2)}) copy-start(f32[4096,256]{1,0:T(8,128)} %fusion.93) | copy-start | bytes 12582916
  702.9 8.2 %copy-start.17 = (bf16[768,256]{1,0:T(8,128)(2,1)S(1)}, bf16[768,256]{1,0:T(8,128)(2,1)}, u32[]{:S(2)}) copy-start(bf16[768,256]{1,0:T(8,128)(2,1)} %param.34) | copy-start | bytes 1179652
  771.8 4.5 copy-start.16
  771.8 4.5 copy-start.40
  776.3 3.1 copy-start.38
  776.3 3.1 copy-start.39
  776.3 24.7 %copy-start.21 = (f32[1024]{0:T(1024)S(1)}, f32[1024]{0:T(1024)}, u32[]{:S(2)}) copy-start(f32[1024]{0:T(1024)} %copy-done.20) | copy-start | bytes 12292
  776.3 24.7 %copy-start.23 = (f32[1024]{0:T(1024)S(1)}, f32[1024]{0:T(1024)}, u32[]{:S(2)}) copy-start(f32[1024]{0:T(1024)} %copy-done.22) | copy-start | bytes 12292
  776.3 24.7 %copy-start.25 = (f32[1024]{0:T(1024)S(1)}, f32[1024]{0:T(1024)}, u32[]{:S(2)}) copy-start(f32[1024]{0:T(1024)} %copy-done.24) | copy-start | bytes 12292
  776.3 24.7 %copy-start.27 = (f32[1024]{0:T(1024)S(1)}, f32[1024]{0:T(1024)}, u32[]{:S(2)}) copy-start(f32[1024]{0:T(1024)} %copy-done.26) | copy-start | bytes 12292
Sparse Core Ops, SparseCore 0:
  9.6 49.0 all-gather.11
  60.9 41.0 all-gather.15
  104.6 97.8 reduce-scatter.2
  204.5 41.0 all-gather.9
  247.6 39.8 all-gather.13
  289.5 39.8 all-gather.17
  331.5 78.6 all-gather.19
  412.4 78.0 all-gather.21
  610.0 44.5 all-gather.23
  656.5 46.3 all-gather.25
  715.8 59.6 reduce-scatter.4
where the time goes:
time: 823 us; the launch traced here: 817 us
  waiting for transfers between devices  436 us (53%)
  matrix products  190 us (23%)
  blocking collectives  62.1 us (8%)
  local copies, waits for them, and re-layouts  61 us (7%)
  other arithmetic  52.4 us (6%)
  between operations  14.8 us (2%)
    reduce_scatter x1, waiting for transfers between devices, per_device(): lax.psum_scatter(jnp.concatenate([jnp.dot(ranked_query, adapter_b, prefer...  90.8 us
    all_gather x1, waiting for transfers between devices, per_device(): lax.all_gather(w_up, 'rows', axis=0, tiled=True)  75 us
    dot_general x8, matrix products, transpose_dot(): lax.dot_general(operand, matrix, (((1,), (1,)), ((), ())), preferred_elem...  65.4 us
    all_gather x1, waiting for transfers between devices, per_device(): group_tokens = lax.all_gather(tokens, 'rank', axis=0, tiled=True)  48.7 us
    all_gather x1, waiting for transfers between devices, per_device(): lax.all_gather(w_down, 'rows', axis=0, tiled=True)  43.9 us
    all_gather x1, waiting for transfers between devices, per_device(): lax.all_gather(out_value, 'rank', axis=0, tiled=True)  41.8 us
    all_gather x1, waiting for transfers between devices, per_device(): lax.all_gather(out_query, 'rank', axis=0, tiled=True)  40.6 us
    psum x1, blocking collectives, per_device(): lax.psum((scale_query_part, scale_value_part), ('rows', 'rank'))  40.5 us
  transfers between devices with their start and end apart: 11, of which 10 were waited for; matrix products, arithmetic and copies ran while one was open for 20% of the time, Pallas kernels for 0%

commit v1 on v0

v1 whole, which is shorter than its diff:
```python
from functools import partial
import math

import jax
import jax.numpy as jnp
from jax import lax
from jax.experimental import pallas as pl
from jax.experimental.pallas import tpu as pltpu
from jax.sharding import PartitionSpec as P

HEADS = 12
HEAD = 64
MESH = pl.DeviceIdType.MESH
epsilon = 1e-05
masked_score = -1e30


def norm_forward(stream, norm_gain, norm_shift):
    centered = stream - jnp.mean(stream, axis=-1, keepdims=True)
    inverse = lax.rsqrt(jnp.mean(centered * centered, axis=-1, keepdims=True) + epsilon)
    normed = centered * inverse
    return (normed * norm_gain + norm_shift, normed, inverse)


def norm_backward(upstream, normed, inverse, norm_gain):
    scaled = upstream * norm_gain
    mean_grad = jnp.mean(scaled, axis=-1, keepdims=True)
    mean_cross = jnp.mean(scaled * normed, axis=-1, keepdims=True)
    return inverse * (scaled - mean_grad - normed * mean_cross)


def dot(a, b):
    return jnp.dot(a, b, preferred_element_type=jnp.float32)


def transpose_dot(operand, matrix):
    return lax.dot_general(
        operand, matrix, (((1,), (1,)), ((), ())), preferred_element_type=jnp.float32
    )


def head_scores(query_heads, key_heads, segment_ids):
    scores = jnp.einsum(
        "qhd,khd->hqk", query_heads, key_heads, preferred_element_type=jnp.float32
    ) / math.sqrt(HEAD)
    same_doc = segment_ids[:, None] == segment_ids[None, :]
    return jnp.where(same_doc[None], scores, masked_score)


def attend_forward(pieces):
    query_heads, key_heads, value_heads, segment_ids = pieces
    scores = head_scores(query_heads, key_heads, segment_ids)
    row_peak = jnp.max(scores, axis=-1, keepdims=True)
    weights = jnp.exp(scores - row_peak)
    row_total = jnp.sum(weights, axis=-1, keepdims=True)
    attention = weights / row_total
    mixture = jnp.einsum(
        "hqk,khd->qhd",
        attention.astype(jnp.bfloat16),
        value_heads,
        preferred_element_type=jnp.float32,
    )
    return (mixture, row_peak + jnp.log(row_total))


def attend_backward(pieces):
    query_heads, key_heads, value_heads, grad_heads, segment_ids, log_total = pieces
    scores = head_scores(query_heads, key_heads, segment_ids)
    attention = jnp.exp(scores - log_total)
    grad_attn = jnp.einsum(
        "qhd,khd->hqk", grad_heads, value_heads, preferred_element_type=jnp.float32
    )
    centre = jnp.sum(attention * grad_attn, axis=-1, keepdims=True)
    grad_scores = (attention * (grad_attn - centre)).astype(jnp.bfloat16)
    grad_query = (
        jnp.einsum("hqk,khd->qhd", grad_scores, key_heads, preferred_element_type=jnp.float32)
        / math.sqrt(HEAD)
    ).astype(jnp.bfloat16)
    grad_key = (
        jnp.einsum("hqk,qhd->khd", grad_scores, query_heads, preferred_element_type=jnp.float32)
        / math.sqrt(HEAD)
    ).astype(jnp.bfloat16)
    grad_value = jnp.einsum(
        "hqk,qhd->khd",
        attention.astype(jnp.bfloat16),
        grad_heads,
        preferred_element_type=jnp.float32,
    ).astype(jnp.bfloat16)
    return (grad_query, grad_key, grad_value)


def gather_kernel(pieces, shards, count, *refs):
    ins, outs = refs[:count], refs[count : 2 * count]
    local_sem, sz, rz, sx, rx, sy, ry, sp, rp, sq, rq = refs[2 * count :]
    row, rank = lax.axis_index("rows"), lax.axis_index("rank")
    z, x, y, c = row // 2, row % 2, rank // 2, rank % 2
    other_z = (z, z + 1 - 2 * (z % 2), (z + 2) % 4, 3 - z)
    to_z = [(other_z[d] * 2 + x, rank) for d in range(4)]
    to_x = (z * 2 + 1 - x, rank)
    to_y = (row, (1 - y) * 2 + c)
    to_core = (row, y * 2 + 1 - c)
    barrier = pltpu.get_barrier_semaphore()
    friends = to_z[1:] + [to_x, to_y, to_core]
    for friend in friends:
        pl.semaphore_signal(barrier, inc=1, device_id=friend, device_id_type=MESH)
    pl.semaphore_wait(barrier, len(friends))

    def rows_of(p, shard, offset, size):
        m, first, total, _ = pieces[p]
        return pl.ds(pl.multiple_of(shard * shards[m] + first + offset, 16), size)

    def plane(p, shard, core):
        unit = pieces[p][2] // 6
        return rows_of(p, shard, 3 * unit * core + unit * y, 2 * unit)

    def half(p, shard, side, core):
        unit = pieces[p][2] // 6
        return rows_of(p, shard, 3 * unit * core + 2 * unit * side, unit)

    def here(p, rows):
        return outs[pieces[p][0]].at[rows]

    def remote(src, dst, send, recv, device):
        return pltpu.make_async_remote_copy(
            src_ref=src, dst_ref=dst, send_sem=send, recv_sem=recv,
            device_id=device, device_id_type=MESH,
        )

    def same(p, rows, send, recv, device):
        return remote(here(p, rows), here(p, rows), send, recv, device)

    def own(p):
        return ins[pieces[p][0]].at[plane(p, 0, c)]

    def shard(j):
        return other_z[j + 1] * 2 + x if j < 3 else other_z[j - 3] * 2 + 1 - x

    def send_z(p, d):
        return remote(own(p), here(p, plane(p, row, c)), sz.at[p, d - 1], rz.at[p, d - 1], to_z[d])

    def recv_z(p, d):
        return same(p, plane(p, shard(d - 1), c), sz.at[p, d - 1], rz.at[p, d - 1], to_z[d])

    def send_x(p, d):
        if d == 0:
            return remote(own(p), here(p, plane(p, row, c)), sx.at[p, 0], rx.at[p, 0], to_x)
        return same(p, plane(p, shard(d - 1), c), sx.at[p, d], rx.at[p, d], to_x)

    def recv_x(p, d):
        return same(p, plane(p, shard(3 + d), c), sx.at[p, d], rx.at[p, d], to_x)

    def send_y(p, j):
        return same(p, half(p, shard(j), y, c), sy.at[p, j], ry.at[p, j], to_y)

    def recv_y(p, j):
        return same(p, half(p, shard(j), 1 - y, c), sy.at[p, j], ry.at[p, j], to_y)

    def send_p(p, j):
        return same(p, plane(p, shard(j), c), sp.at[p, j], rp.at[p, j], to_core)

    def recv_p(p, j):
        return same(p, plane(p, shard(j), 1 - c), sp.at[p, j], rp.at[p, j], to_core)

    def send_q(p, j):
        return same(p, half(p, shard(j), 1 - y, c), sq.at[p, j], rq.at[p, j], to_core)

    def recv_q(p, j):
        return same(p, half(p, shard(j), 1 - y, 1 - c), sq.at[p, j], rq.at[p, j], to_core)

    total = len(pieces)
    ahead = 2
    local = [
        pltpu.make_async_copy(
            ins[m], outs[m].at[pl.ds(pl.multiple_of(row * shards[m], 16), shards[m])], local_sem.at[m]
        )
        for m in range(count)
    ]
    for copy in local:
        copy.start()

    def launch(p):
        for d in (1, 2, 3):
            send_z(p, d).start()
        send_x(p, 0).start()

    for p in range(ahead):
        launch(p)
    for t in range(total + 2):
        if t < total:
            recv_x(t, 0).wait_recv()
            send_y(t, 3).start()
            send_p(t, 3).start()
            for d in (1, 2, 3):
                recv_z(t, d).wait_recv()
                send_x(t, d).start()
                send_y(t, d - 1).start()
                send_p(t, d - 1).start()
        if t + ahead < total:
            launch(t + ahead)
        if 0 <= t - 1 < total:
            for d in (1, 2, 3):
                recv_x(t - 1, d).wait_recv()
                send_y(t - 1, 3 + d).start()
                send_p(t - 1, 3 + d).start()
        if 0 <= t - 2 < total:
            for j in range(7):
                recv_y(t - 2, j).wait_recv()
                send_q(t - 2, j).start()
    for p in range(total):
        for j in range(7):
            recv_p(p, j).wait_recv()
            recv_q(p, j).wait_recv()
    for copy in local:
        copy.wait()
    for p in range(total):
        for d in (1, 2, 3):
            send_z(p, d).wait_send()
        for d in range(4):
            send_x(p, d).wait_send()
        for j in range(7):
            send_y(p, j).wait_send()
            send_p(p, j).wait_send()
            send_q(p, j).wait_send()


def gather_weights(mesh_shape, weights):
    if mesh_shape != (8, 4) or any(w.shape[0] % 96 for w in weights):
        return [lax.all_gather(w, "rows", axis=0, tiled=True) for w in weights]
    shards = [w.shape[0] for w in weights]
    pieces = []
    for m, w in enumerate(weights):
        parts = max(1, w.shape[0] // 192)
        for part in range(parts):
            pieces.append((m, part * (w.shape[0] // parts), w.shape[0] // parts, w.shape[1]))
    count, total = len(weights), len(pieces)
    sem = pltpu.SemaphoreType.DMA
    anywhere = pl.BlockSpec(memory_space=pl.ANY)
    return pl.pallas_call(
        partial(gather_kernel, pieces, shards, count),
        out_shape=[
            jax.ShapeDtypeStruct((w.shape[0] * mesh_shape[0], w.shape[1]), w.dtype) for w in weights
        ],
        in_specs=[anywhere] * count,
        out_specs=[anywhere] * count,
        scratch_shapes=[sem((count,))] + [sem((total, n)) for n in (3, 3, 4, 4, 7, 7, 7, 7, 7, 7)],
        compiler_params=pltpu.CompilerParams(collective_id=0, has_side_effects=True),
    )(*weights)


def per_device(
    mesh_shape,
    tokens,
    w_query,
    w_key,
    w_value,
    w_out,
    w_up,
    w_down,
    gain_one,
    shift_one,
    gain_two,
    shift_two,
    adapter_a,
    adapter_b,
    query_rank_scale,
    value_rank_scale,
    query_out_scale,
    value_out_scale,
    segments,
    cotangent,
):
    local_rows, width = tokens.shape
    rows_here, row_length = segments.shape
    rank_here = adapter_a.shape[1]

    def split_heads(tensor_rows):
        return tensor_rows.reshape(rows_here, row_length, HEADS, HEAD)

    full_a = lax.all_gather(adapter_a, "rank", axis=1, tiled=True)
    full_b = lax.all_gather(adapter_b, "rank", axis=0, tiled=True)
    scales = lax.all_gather(
        jnp.stack([query_rank_scale, value_rank_scale]), "rank", axis=1, tiled=True
    )
    full_key, full_query, full_value, full_out, full_up, full_down = gather_weights(
        mesh_shape, [w_key, w_query, w_value, w_out, w_up, w_down]
    )
    merged_query = (
        full_query + dot((full_a * scales[0]), full_b) * query_out_scale.astype(jnp.float32)
    ).astype(jnp.bfloat16)
    merged_value = (
        full_value + dot((full_a * scales[1]), full_b) * value_out_scale.astype(jnp.float32)
    ).astype(jnp.bfloat16)
    queries = dot(tokens, merged_query).astype(jnp.bfloat16)
    key_rows = dot(tokens, full_key).astype(jnp.bfloat16)
    values = dot(tokens, merged_value).astype(jnp.bfloat16)
    mixture, log_total = lax.map(
        attend_forward, (split_heads(queries), split_heads(key_rows), split_heads(values), segments)
    )
    mixture_low = mixture.reshape(local_rows, width).astype(jnp.bfloat16)
    first_sum = tokens.astype(jnp.float32) + dot(mixture_low, full_out)
    normed_out, normed_one, inverse_one = norm_forward(first_sum, gain_one, shift_one)
    up_proj = dot(normed_out.astype(jnp.bfloat16), full_up)
    activated = jax.nn.gelu(up_proj, approximate=False).astype(jnp.bfloat16)
    second_sum = normed_out + dot(activated, full_down)
    layer_out, normed_two, inverse_two = norm_forward(second_sum, gain_two, shift_two)
    grad_second = norm_backward(cotangent.astype(jnp.float32), normed_two, inverse_two, gain_two)
    grad_act = transpose_dot(grad_second.astype(jnp.bfloat16), full_down)
    gelu_grad = jax.vjp(partial(jax.nn.gelu, approximate=False), up_proj)[1](grad_act)[0]
    grad_normed = grad_second + transpose_dot(gelu_grad.astype(jnp.bfloat16), full_up)
    grad_first = norm_backward(grad_normed, normed_one, inverse_one, gain_one)
    grad_mixture = transpose_dot(grad_first.astype(jnp.bfloat16), full_out).astype(jnp.bfloat16)
    grad_query, grad_key, grad_value = lax.map(
        attend_backward,
        (
            split_heads(queries),
            split_heads(key_rows),
            split_heads(values),
            split_heads(grad_mixture),
            segments,
            log_total,
        ),
    )
    grad_query = grad_query.reshape(local_rows, width)
    grad_key = grad_key.reshape(local_rows, width)
    grad_value = grad_value.reshape(local_rows, width)

    def token_product(grad):
        return lax.dot_general(
            tokens, grad, (((0,), (0,)), ((), ())), preferred_element_type=jnp.float32
        ).astype(jnp.bfloat16)

    def through_a(grad):
        return lax.dot_general(
            full_a, token_product(grad), (((0,), (0,)), ((), ())), preferred_element_type=jnp.float32
        )

    with_b_query = through_a(grad_query) * full_b.astype(jnp.float32)
    with_b_value = through_a(grad_value) * full_b.astype(jnp.float32)
    small = jnp.concatenate(
        [
            jnp.sum(with_b_query * query_out_scale.astype(jnp.float32), axis=1),
            jnp.sum(with_b_value * value_out_scale.astype(jnp.float32), axis=1),
            jnp.sum(with_b_query * scales[0].astype(jnp.float32)[:, None], axis=0),
            jnp.sum(with_b_value * scales[1].astype(jnp.float32)[:, None], axis=0),
        ]
    )
    small = lax.psum(small, ("rows", "rank"))
    all_ranks = full_b.shape[0]
    mine = lax.axis_index("rank") * rank_here
    input_sum = (
        grad_first
        + transpose_dot(grad_query, merged_query)
        + transpose_dot(grad_key, full_key)
        + transpose_dot(grad_value, merged_value)
    )
    return (
        layer_out.astype(jnp.bfloat16),
        input_sum.astype(jnp.bfloat16),
        lax.dynamic_slice(small, (mine,), (rank_here,)),
        lax.dynamic_slice(small, (all_ranks + mine,), (rank_here,)),
        small[2 * all_ranks : 2 * all_ranks + width],
        small[2 * all_ranks + width :],
    )


def solution(mesh):
    return jax.shard_map(
        partial(per_device, (mesh.shape["rows"], mesh.shape["rank"])),
        mesh=mesh,
        in_specs=(
            P(("rows", "rank"), None),
            P("rows", None),
            P("rows", None),
            P("rows", None),
            P("rows", None),
            P("rows", None),
            P("rows", None),
            P(),
            P(),
            P(),
            P(),
            P(None, "rank"),
            P("rank", None),
            P("rank"),
            P("rank"),
            P(),
            P(),
            P(("rows", "rank"), None),
            P(("rows", "rank"), None),
        ),
        out_specs=(
            P(("rows", "rank"), None),
            P(("rows", "rank"), None),
            P("rank"),
            P("rank"),
            P(),
            P(),
        ),
        check_vma=False,
    )
```

time: 823 us -> 398 us (0.48)
  waiting for transfers between devices: 436 us -> 0.7 us
  Pallas kernels: 0 us -> 75.4 us
  other arithmetic: 52.4 us -> 29.2 us
  matrix products: 190 us -> 174 us
  blocking collectives: 62.1 us -> 46.3 us
    all_gather x9 -> x2, waiting for transfers between devices: 340 us -> 0.01 us  [the longest x1 0.01 us: per_device(): full_a = lax.all_gather(adapter_a, 'rank', axis=1, tiled=True)]
    reduce_scatter x2 -> x0, waiting for transfers between devices: 90.8 us -> none  [the longest x1 90.8 us: per_device(): lax.psum_scatter(jnp.concatenate([jnp.dot(ranked_query, adapter_b, prefer...]
    pallas_call x0 -> x1, Pallas kernels: none -> 75.4 us  [gather_weights(): pl.pallas_call(partial(gather_kernel, pieces, shards, count), out_shape=[...]
    dot_general x8 -> x5, matrix products: 65.4 us -> 35.6 us  [transpose_dot(): lax.dot_general(operand, matrix, (((1,), (1,)), ((), ())), preferred_elem...]
    psum x2 -> x1, blocking collectives: 62.1 us -> 41.3 us  [per_device(): small = lax.psum(small, ('rows', 'rank'))]
    dot_general x9 -> x10, matrix products: 77.5 us -> 91.8 us  [the longest x8 78.3 us: dot(): return jnp.dot(a, b, preferred_element_type=jnp.float32)]
    unnamed x74 -> x95, local copies, waits for them, and re-layouts: 14.4 us -> 18.5 us
  transfers between devices with their start and end apart: 11 -> 2, of which waited for: 10 -> 0; matrix products, arithmetic and copies ran while one was open for 20% -> 4% of each run, Pallas kernels for 0% -> 19%
where the time goes in v1:
time: 398 us; the launch traced here: 396 us
  matrix products  174 us (44%)
  Pallas kernels  75.4 us (19%)
  local copies, waits for them, and re-layouts  54.1 us (14%)
  blocking collectives  46.3 us (12%)
  other arithmetic  29.2 us (7%)
  between operations  14.9 us (4%)
    dot_general x8, matrix products, dot(): return jnp.dot(a, b, preferred_element_type=jnp.float32)  78.3 us
    pallas_call x1, Pallas kernels, gather_weights(): pl.pallas_call(partial(gather_kernel, pieces, shards, count), out_shape=[...  75.4 us
    psum x1, blocking collectives, per_device(): small = lax.psum(small, ('rows', 'rank'))  41.3 us
    dot_general x5, matrix products, transpose_dot(): lax.dot_general(operand, matrix, (((1,), (1,)), ((), ())), preferred_elem...  35.6 us
    unnamed x95, local copies, waits for them, and re-layouts  18.5 us
    convert_element_type x2, other arithmetic, attend_backward(): grad_scores = (attention * (grad_attn - centre)).astype(jnp.bfloat16)  14.2 us
    dot_general x2, matrix products, attend_backward(): jnp.einsum('qhd,khd->hqk', grad_heads, value_heads, preferred_element_typ...  13.8 us
    dot_general x2, matrix products, through_a(): lax.dot_general(full_a, token_product(grad), (((0,), (0,)), ((), ())), pr...  13.5 us
  transfers between devices with their start and end apart: 2, of which 0 were waited for; matrix products, arithmetic and copies ran while one was open for 4% of the time, Pallas kernels for 19%

profile of v1, /device:TPU:0, one launch (start us, length us, event | category | flops | bytes accessed | tf_op | source)
XLA Modules:
  0.0 395.7 jit_solution(3842245262390822104)
XLA Ops:
  8.0 2.0 copy.49
  12.8 2.6 copy.48
  15.4 75.4 %shard_map.226 = (bf16[768,768]{1,0:T(8,128)(2,1)}, bf16[768,768]{1,0:T(8,128)(2,1)}, bf16[768,768]{1,0:T(8,128)(2,1)}, bf16[768,768]{1,0:T(8,128)(2,1)}, bf16[7...) custom-call(bf16[96,768]{1,0:T(8,128)(2,1)} %refs_0_.1, bf16[96,768]{1,0:T(8,128)(2,1)} %refs_1_.1, ...), custom_call_target="tpu_custom_call" | custom-call | tf_op jit(solution)/shard_map/pallas_call | solution.py:238
  90.7 2.7 fusion.79
  93.4 1.2 reshape.182
  95.0 2.7 copy.54
  97.7 5.1 %all_gather.10 = bf16[2,1024]{1,0:T(2,128)(2,1)S(1)} all-gather(bf16[2,256]{1,0:T(2,128)(2,1)S(1)} %pad_maximum_fusion.1), channel_id=1, replica_groups=mesh['rows'=8,'rank'=4] {'rank'}, dimensions={1}, use_global_device_ids=true | all-gather | bytes 5120 | tf_op jit(solution)/shard_map/all_gather | solution.py:281
  104.0 3.4 add_convert_fusion.5
  107.4 1.0 copy-done.20
  108.4 2.6 fusion.77
  111.0 3.1 reshape.180
  114.2 1.5 copy.50
  115.8 0.8 copy-done.40
  116.6 2.8 add_convert_fusion.4
  119.4 1.0 copy-done.46
  120.5 1.4 fusion.78
  121.9 2.4 reshape.181
  124.3 1.7 copy.51
  126.0 20.8 %while.26 = (s32[]{:T(128)}, bf16[2,512,12,64]{1,3,2,0:T(8,128)(2,1)}, f32[2,12,512,1]{2,1,3,0:T(8,128)S(1)}, bf16[2,512,12,64]{1,3,2,0:T(8,128)(2,1)}, s32[2,51...) while((s32[]{:T(128)}, ...), condition=%wide.region_3.4_spmd, body=%wide.region_0.3_spmd.sunk | while | flops 843311104 | bytes 42958940 | solution.py:296
  126.3 2.1 fusion.146
  128.4 2.6 fusion.147
  131.0 5.5 %bitcast_dynamic-update-slice_fusion.4 = bf16[2,512,12,64]{1,3,2,0:T(8,128)(2,1)} fusion(bf16[2,512,12,64]{1,3,2,0:T(8,128)(2,1)} %get-tuple-element.346, s32[]{:T(128)} %get-tuple-element.345, f32[12,512,512]{1,2,0:T(8,128)S(1)} %get-tuple-element.323, f32[12,512]{1,0:T(8,128)S(1)} %fusion.147, f32[12,512]{1,0:T(8,128)S(1)} %get-tuple-element.324, ...), kind=kOutput, calls=%fused_computation.6.clone.1 | convolution fusion | flops 418381824 | bytes 15254528 | tf_op jit(solution)/shard_map/while/body/eval_jaxpr/hqk,khd->qhd/dot_general | solution.py:57
  136.7 2.1 fusion.146
  138.7 2.6 fusion.147
  141.3 5.5 %bitcast_dynamic-update-slice_fusion.4 = bf16[2,512,12,64]{1,3,2,0:T(8,128)(2,1)} fusion(bf16[2,512,12,64]{1,3,2,0:T(8,128)(2,1)} %get-tuple-element.346, s32[]{:T(128)} %get-tuple-element.345, f32[12,512,512]{1,2,0:T(8,128)S(1)} %get-tuple-element.323, f32[12,512]{1,0:T(8,128)S(1)} %fusion.147, f32[12,512]{1,0:T(8,128)S(1)} %get-tuple-element.324, ...), kind=kOutput, calls=%fused_computation.6.clone.1 | convolution fusion | flops 418381824 | bytes 15254528 | tf_op jit(solution)/shard_map/while/body/eval_jaxpr/hqk,khd->qhd/dot_general | solution.py:57
  146.8 3.2 copy.53
  150.4 1.6 fusion.95
  153.0 46.5 %fusion.54 = (f32[1024,3072]{1,0:T(8,128)}, f32[1024,3072]{1,0:T(8,128)}) fusion(bf16[768,3072]{1,0:T(8,128)(2,1)S(1)} %bitcast.191, f32[1024,768]{0,1:T(8,128)S(1)} %get-tuple-element.217, f32[768]{0:T(1024)S(1)} %copy-done.44, f32[768]{0:T(1024)S(1)} %copy-done.45, f32[1024]{0:T(1024)S(1)} %add_rsqrt_fusion.1, f32[1024]{0:T(1024)S(1)} %broadcast_multiply_fusion.5), kind=kOutput, calls=%fused_computation.63 | convolution fusion | flops 5030805504 | bytes 33044480 | tf_op jit(solution)/shard_map/dot_general | solution.py:33
  199.5 17.3 %fusion.96 = (f32[1024]{0:T(1024)S(1)}, f32[1024,768]{0,1:T(8,128)}) fusion(bf16[3072,768]{1,0:T(8,128)(2,1)} %get-tuple-element.110, f32[1024,3072]{1,0:T(8,128)} %get-tuple-element.218, f32[1024,3072]{1,0:T(8,128)} %get-tuple-element.219, f32[768]{0:T(1024)S(1)} %copy-done.44, f32[768]{0:T(1024)S(1)} %copy-done.45, f32[1024]{0:T(1024)S(1)} %add_rsqrt_fusion.1, ...), kind=kOutput, calls=%fused_computation.150 | convolution fusion | flops 4845992960 | bytes 36194304 | tf_op jit(solution)/shard_map/dot_general | solution.py:33
  216.8 2.4 multiply_reduce_fusion.7
  219.6 3.6 fusion.63
  223.3 22.8 %fusion.92 = (f32[1024]{0:T(1024)S(1)}, f32[1024]{0:T(1024)S(1)}, f32[1024,768]{0,1:T(8,128)}) fusion(f32[1024]{0:T(1024)S(1)} %add_rsqrt_fusion.1, f32[1024,768]{0,1:T(8,128)} %copy-done.3, f32[1024]{0:T(1024)S(1)} %broadcast_multiply_fusion.5, f32[768]{0:T(1024)S(1)} %copy-done.45, bf16[768,3072]{1,0:T(8,128)(2,1)} %get-tuple-element.109, ...), kind=kOutput, calls=%fused_computation.146 | convolution fusion | flops 9726588928 | bytes 45651968 | tf_op jit(solution)/shard_map/dot_general | solution.py:37
  246.1 6.3 %convolution_convert_fusion = bf16[1024,768]{1,0:T(8,128)(2,1)} fusion(bf16[768,768]{1,0:T(8,128)(2,1)} %get-tuple-element.108, f32[1024,768]{0,1:T(8,128)} %get-tuple-element.222, f32[1024,768]{0,1:T(8,128)} %copy-done.3, f32[1024]{0:T(1024)S(1)} %broadcast_multiply_fusion, f32[1024]{0:T(1024)S(1)} %broadcast_multiply_fusion.1, ...), kind=kOutput, calls=%fused_computation.107 | convolution fusion | flops 1214251008 | bytes 9060352 | tf_op jit(solution)/shard_map/dot_general | solution.py:37
  252.5 2.6 copy.55
  255.1 3.8 reshape.183
  259.0 2.9 copy.58
  261.9 49.4 %while.27 = (s32[]{:T(128)}, bf16[2,512,12,64]{1,3,2,0:T(8,128)(2,1)}, bf16[2,512,12,64]{1,3,2,0:T(8,128)(2,1)}, bf16[2,512,12,64]{1,3,2,0:T(8,128)(2,1)}, bf16[...) while((s32[]{:T(128)}, ...), condition=%wide.region_14.15_spmd, body=%wide.region_12.14_spmd.sunk | while | flops 2062673920 | bytes 147524944 | solution.py:312
  262.3 1.8 fusion.156
  264.4 6.9 %multiply_reduce_fusion.10 = (f32[12,512]{1,0:T(8,128)S(1)}, f32[12,512,512]{1,2,0:T(8,128)}) fusion(f32[12,512,512]{1,2,0:T(8,128)S(1)} %fusion.156, f32[12,512]{1,0:T(8,128)S(1)} %dynamic-slice_bitcast_fusion.2, pred[512,512]{0,1:T(8,128)(4,1)S(1)} %broadcast_compare_fusion.5, bf16[2,512,12,64]{1,3,2,0:T(8,128)(2,1)S(1)} %copy-done, ...), kind=kOutput, calls=%fused_computation.22.clone.1 | convolution fusion | flops 418375680 | bytes 27059200 | tf_op jit(solution)/shard_map/while/body/eval_jaxpr/qhd,khd->hqk/dot_general | solution.py:70
  271.3 7.1 %multiply_convert_fusion.8 = bf16[12,512,512]{1,2,0:T(8,128)(2,1)S(1)} fusion(f32[12,512,512]{1,2,0:T(8,128)} %get-tuple-element.335, f32[12,512,512]{1,2,0:T(8,128)S(1)} %fusion.156, f32[12,512]{1,0:T(8,128)S(1)} %get-tuple-element.336, f32[12,512]{1,0:T(8,128)S(1)} %dynamic-slice_bitcast_fusion.2, pred[512,512]{0,1:T(8,128)(4,1)S(1)} %broadcast_compare_fusion.5), kind=kLoop, calls=%fused_computation.21.clone.1 | loop fusion | flops 18874368 | bytes 31768576 | tf_op jit(solution)/shard_map/while/body/eval_jaxpr/convert_element_type | solution.py:74
  278.4 2.0 fusion.158
  280.5 1.1 fusion.157
  281.6 1.2 copy-done.14
  282.8 3.9 fusion.159
  286.7 1.8 fusion.156
  288.8 6.9 %multiply_reduce_fusion.10 = (f32[12,512]{1,0:T(8,128)S(1)}, f32[12,512,512]{1,2,0:T(8,128)}) fusion(f32[12,512,512]{1,2,0:T(8,128)S(1)} %fusion.156, f32[12,512]{1,0:T(8,128)S(1)} %dynamic-slice_bitcast_fusion.2, pred[512,512]{0,1:T(8,128)(4,1)S(1)} %broadcast_compare_fusion.5, bf16[2,512,12,64]{1,3,2,0:T(8,128)(2,1)S(1)} %copy-done, ...), kind=kOutput, calls=%fused_computation.22.clone.1 | convolution fusion | flops 418375680 | bytes 27059200 | tf_op jit(solution)/shard_map/while/body/eval_jaxpr/qhd,khd->hqk/dot_general | solution.py:70
  295.7 7.1 %multiply_convert_fusion.8 = bf16[12,512,512]{1,2,0:T(8,128)(2,1)S(1)} fusion(f32[12,512,512]{1,2,0:T(8,128)} %get-tuple-element.335, f32[12,512,512]{1,2,0:T(8,128)S(1)} %fusion.156, f32[12,512]{1,0:T(8,128)S(1)} %get-tuple-element.336, f32[12,512]{1,0:T(8,128)S(1)} %dynamic-slice_bitcast_fusion.2, pred[512,512]{0,1:T(8,128)(4,1)S(1)} %broadcast_compare_fusion.5), kind=kLoop, calls=%fused_computation.21.clone.1 | loop fusion | flops 18874368 | bytes 31768576 | tf_op jit(solution)/shard_map/while/body/eval_jaxpr/convert_element_type | solution.py:74
  302.8 2.0 fusion.158
  304.9 1.1 fusion.157
  306.1 1.2 copy-done.14
  307.2 3.9 fusion.159
  311.3 3.1 copy.64
  314.9 1.6 copy.60
  317.0 3.0 fusion.99
  320.0 6.4 %fusion.83 = f32[768,1024]{1,0:T(8,128)} fusion(bf16[768,1024]{1,0:T(8,128)(2,1)} %all-gather.3.cloned.1.call-done, bf16[1024,768]{0,1:T(8,128)(2,1)S(1)} %bitcast.178, bf16[1024,768]{1,0:T(8,128)(2,1)S(1)} %copy-done.12), kind=kOutput, calls=%fused_computation.129 | convolution fusion | flops 2416508928 | bytes 7864320 | tf_op jit(solution)/shard_map/dot_general | solution.py:333
  326.5 7.0 %multiply_reduce_fusion.4 = (f32[1024]{0:T(1024)S(1)}, f32[768]{0:T(1024)S(1)}, f32[768]{0:T(1024)S(1)}, f32[1024]{0:T(1024)S(1)}) fusion(bf16[1024,768]{0,1:T(8,128)(2,1)} %all-gather.5.cloned.1.call-done, f32[768]{0:T(1024)S(1)} %copy-done.36, f32[1024]{0:T(1024)S(1)} %copy-done.37, f32[1024]{0:T(1024)S(1)} %copy-done.38, f32[768,1024]{1,0:T(8,128)} %fusion.83, ...), kind=kOutput, calls=%fused_computation.87 | convolution fusion | flops 2425156096 | bytes 9465856 | tf_op jit(solution)/shard_map/dot_general | solution.py:333
  333.5 41.3 %psum.7 = f32[3584]{0:T(1024)S(1)} all-reduce(f32[3584]{0:T(1024)S(1)} %pad_maximum_fusion), channel_id=1, replica_groups=mesh['rows'=8,'rank'=4] {'rows','rank'}, use_global_device_ids=true, to_apply=%region_19.20 | all-reduce | flops 3584 | bytes 28672 | tf_op jit(solution)/shard_map/psum | solution.py:347
  375.4 3.1 copy.62
  379.0 1.4 fusion.100
  380.9 0.9 copy-done.7
  381.9 0.9 copy-done.8
  382.8 2.0 add_convert_fusion.2
  384.8 1.6 copy.67
  386.4 1.6 copy.66
  (155 shorter events, 11.1 us)
Async XLA Ops:
  7.2 96.8 %all-gather.3.cloned.1.call-start = ((), (), s32[]{:S(2)}) async-start(), calls=%async_computation | async-start | bytes 1966080 | tf_op jit(solution)/shard_map/all_gather | solution.py:279
  7.9 82.8 %copy-start.9 = (bf16[1024,768]{1,0:T(8,128)(2,1)S(1)}, bf16[1024,768]{1,0:T(8,128)(2,1)}, u32[]{:S(2)}) copy-start(bf16[1024,768]{1,0:T(8,128)(2,1)} %param.23) | copy-start | bytes 4718596
  7.9 96.0 %all-gather.5.cloned.1.call-start = ((), (), s32[]{:S(2)}) async-start(), calls=%async_computation.1 | async-start | bytes 1966080 | tf_op jit(solution)/shard_map/all_gather | solution.py:280
  12.1 91.9 %copy-start.33 = (f32[768]{0:T(1024)}, f32[768]{0:T(1024)S(1)}, u32[]{:S(2)}) copy-start(f32[768]{0:T(1024)S(1)} %convert_element_type.129) | copy-start | bytes 9220
  12.8 102.8 %copy-start.35 = (f32[768]{0:T(1024)}, f32[768]{0:T(1024)S(1)}, u32[]{:S(2)}) copy-start(f32[768]{0:T(1024)S(1)} %convert_element_type.134) | copy-start | bytes 9220
  95.0 9.0 %copy-start.43 = (bf16[768,768]{1,0:T(8,128)(2,1)S(1)}, bf16[768,768]{1,0:T(8,128)(2,1)}, u32[]{:S(2)}) copy-start(bf16[768,768]{1,0:T(8,128)(2,1)} %get-tuple-element.104) | copy-start | bytes 3538948
  104.0 4.5 %copy-start.10 = (bf16[1024,768]{1,0:T(8,128)(2,1)S(1)}, bf16[1024,768]{1,0:T(8,128)(2,1)}, u32[]{:S(2)}) copy-start(bf16[1024,768]{1,0:T(8,128)(2,1)} %param.23) | copy-start | bytes 4718596
  107.4 1.0 copy-start.20
  114.1 1.7 copy-start.39
  114.1 2.4 copy-start.40
  116.6 3.9 copy-start.11
  119.4 1.0 copy-start.46
  121.9 4.1 %copy-start.22 = (s32[2,512]{1,0:T(2,128)S(1)}, s32[2,512]{1,0:T(2,128)}, u32[]{:S(2)}) copy-start(s32[2,512]{1,0:T(2,128)} %param.40) | copy-start | bytes 12292
  146.8 3.6 copy-start.18
  146.8 3.6 copy-start.42
  150.4 2.2 slice-start
  150.4 2.3 slice-start.1
  152.0 47.5 %copy-start.3 = (f32[1024,768]{0,1:T(8,128)}, f32[1024,768]{0,1:T(8,128)S(1)}, u32[]{:S(2)}) copy-start(f32[1024,768]{0,1:T(8,128)S(1)} %get-tuple-element.217) | copy-start | bytes 9437188
  152.0 0.9 copy-start.44
  152.0 0.9 copy-start.45
  152.1 94.1 %copy-start.23 = (f32[1024]{0:T(1024)}, f32[1024]{0:T(1024)S(1)}, u32[]{:S(2)}) copy-start(f32[1024]{0:T(1024)S(1)} %broadcast_multiply_fusion.5) | copy-start | bytes 12292
  152.5 93.7 %copy-start.25 = (f32[1024]{0:T(1024)}, f32[1024]{0:T(1024)S(1)}, u32[]{:S(2)}) copy-start(f32[1024]{0:T(1024)S(1)} %add_rsqrt_fusion.1) | copy-start | bytes 12292
  216.8 2.8 copy-start.5
  216.8 2.8 copy-start.31
  216.8 2.8 copy-start.32
  246.1 6.4 %copy-start.27 = (f32[1024]{0:T(1024)}, f32[1024]{0:T(1024)S(1)}, u32[]{:S(2)}) copy-start(f32[1024]{0:T(1024)S(1)} %broadcast_multiply_fusion) | copy-start | bytes 12292
  246.1 6.4 %copy-start.29 = (f32[1024]{0:T(1024)}, f32[1024]{0:T(1024)S(1)}, u32[]{:S(2)}) copy-start(f32[1024]{0:T(1024)S(1)} %broadcast_multiply_fusion.1) | copy-start | bytes 12292
  262.3 2.1 copy-start
  262.3 2.1 copy-start.1
  271.3 7.1 %copy-start.16 = (bf16[2,512,12,64]{1,3,2,0:T(8,128)(2,1)S(1)}, bf16[2,512,12,64]{1,3,2,0:T(8,128)(2,1)}, u32[]{:S(2)}) copy-start(bf16[2,512,12,64]{1,3,2,0:T(8,128)(2,1)} %get-tuple-element.374) | copy-start | bytes 4718596 | tf_op jit(solution)/shard_map/while
  278.4 2.0 copy-start.13
  280.5 1.2 copy-start.17
  280.5 2.3 copy-start.2
  281.6 1.2 copy-start.14
  286.7 2.1 copy-start
  286.7 2.1 copy-start.1
  295.7 7.1 %copy-start.16 = (bf16[2,512,12,64]{1,3,2,0:T(8,128)(2,1)S(1)}, bf16[2,512,12,64]{1,3,2,0:T(8,128)(2,1)}, u32[]{:S(2)}) copy-start(bf16[2,512,12,64]{1,3,2,0:T(8,128)(2,1)} %get-tuple-element.374) | copy-start | bytes 4718596 | tf_op jit(solution)/shard_map/while
  302.8 2.0 copy-start.13
  304.9 1.2 copy-start.17
  304.9 2.3 copy-start.2
  306.0 1.2 copy-start.14
  311.3 3.6 copy-start.15
  314.9 2.1 copy-start.47
  316.9 3.1 copy-start.19
  317.0 3.1 copy-start.12
  320.0 6.5 %copy-start.34 = (f32[768]{0:T(1024)S(1)}, f32[768]{0:T(1024)}, u32[]{:S(2)}) copy-start(f32[768]{0:T(1024)} %copy-done.33) | copy-start | bytes 9220
  320.0 6.5 %copy-start.36 = (f32[768]{0:T(1024)S(1)}, f32[768]{0:T(1024)}, u32[]{:S(2)}) copy-start(f32[768]{0:T(1024)} %copy-done.35) | copy-start | bytes 9220
  320.0 6.5 %copy-start.37 = (f32[1024]{0:T(1024)S(1)}, f32[1024]{0:T(1024)}, u32[]{:S(2)}) copy-start(f32[1024]{0:T(1024)} %convert_element_type.154) | copy-start | bytes 12292
  320.0 6.5 %copy-start.38 = (f32[1024]{0:T(1024)S(1)}, f32[1024]{0:T(1024)}, u32[]{:S(2)}) copy-start(f32[1024]{0:T(1024)} %convert_element_type.155) | copy-start | bytes 12292
  375.4 3.6 copy-start.41
  378.5 1.9 copy-start.21
  379.0 2.0 copy-start.4
  379.0 2.9 copy-start.7
  379.0 3.8 copy-start.8
  379.0 3.8 copy-start.24
  379.0 3.8 copy-start.26
  379.0 3.8 copy-start.28
  379.0 3.8 copy-start.30
  384.8 1.6 copy-start.6
Sparse Core Ops, SparseCore 0:
  9.6 26.4 all-gather.2
  37.6 24.9 all-gather.4
